TPU v7x, 32 devices: a whole 2x2x4 slice. The times are simulated.
32 devices in a mesh: groups: 2 (over x), seq: 16 (over z, y, core).
Axes of the slice: x: 2, y: 2, z: 4, core: 2. Of those that a mesh axis runs over, the one named last changes fastest.
Arguments:
- queries: bfloat16 [128, 8192], P(('groups', 'seq')), parts along dimension 0, may hold values from -15 to 15
- draft_keys: bfloat16 [128, 1024], P(('groups', 'seq')), parts along dimension 0, may hold values from -16 to 16
- draft_values: bfloat16 [128, 1024], P(('groups', 'seq')), parts along dimension 0, may hold values from -6 to 6
- parents: int32 [128], P(('groups', 'seq')), parts along dimension 0, may hold values from -1 to 2, as said below
- private_keys: bfloat16 [32, 1024, 1024], P(('groups', 'seq')), parts along dimension 0, may hold values from -8 to 8
- private_values: bfloat16 [32, 1024, 1024], P(('groups', 'seq')), parts along dimension 0, may hold values from -6 to 6
- priv_lengths: int32 [32], P(('groups', 'seq')), parts along dimension 0, may hold values from 1 to 1024, as said below
- prefix_keys: bfloat16 [32, 16384, 128], P(('groups', 'seq')), parts along dimension 0, may hold values from -8 to 8
- prefix_values: bfloat16 [32, 16384, 128], P(('groups', 'seq')), parts along dimension 0, may hold values from -6 to 6
- out_weight: bfloat16 [8192, 8192], P(None, 'seq'), may hold values from -0.0625 to 0.0625
Outputs:
- output: float32 [128, 8192], P(('groups', 'seq')), parts along dimension 0
There are 2 independent parts, one for each index of `groups`. A program takes and returns all parts, laid end to end along the dimension named above; an argument that names none is the same for every part. Nothing has to cross between parts.
Inputs may be any that keep to these rules, and one draw needn't show every extreme that they name: parents[r * 4 + i] is the draft of request r that draft i extends, always smaller than i; -1 means draft i extends the cached context directly. Request r's live private slots are its first priv_lengths[r] slots; some request has all 1024.
All inputs are finite; a program needn't handle non-finite values.
Results may differ from a plain program's by a relative error of at most 0.0034.
Values may be sent and summed in bfloat16 or wider, within the bound.
A program may use at most 192 MiB of HBM per device.

v0:
```python
import jax
import jax.numpy as jnp
from jax import lax
from jax.sharding import PartitionSpec as P

HEADS = 64
KVH = 8
HD = 128
DRAFT = 4
PRIV = 1024


def from_partner(array, axis, bit):
    return lax.ppermute(array, axis, [(i, i ^ 1 << bit) for i in range(lax.axis_size(axis))])


def tree_visible(parents):
    parent_rows = parents.reshape(-1, DRAFT)
    positions = jnp.arange(DRAFT, dtype=jnp.int32)
    visible = jnp.broadcast_to(
        positions[:, None] == positions[None, :], (parent_rows.shape[0], DRAFT, DRAFT)
    )
    ancestor = parent_rows
    for repeat_step in range(DRAFT - 1):
        matched = ancestor[:, :, None] == positions[None, None, :]
        visible = visible | matched
        lifted = jnp.sum(jnp.where(matched, parent_rows[:, None, :], 0), axis=2)
        ancestor = jnp.where(ancestor >= 0, lifted, -1)
    return visible


def merge_pair(first, second):
    first_max, first_sum, first_out = first
    second_max, second_sum, second_out = second
    peak_max = jnp.maximum(first_max, second_max)
    first_factor = jnp.exp(first_max - peak_max)
    second_factor = jnp.exp(second_max - peak_max)
    joined_sum = first_factor * first_sum + second_factor * second_sum
    joined_out = first_factor[..., None] * first_out + second_factor[..., None] * second_out
    return (peak_max, joined_sum, joined_out)


def shards(
    queries,
    draft_keys,
    draft_values,
    parents,
    private_keys,
    private_values,
    priv_lengths,
    prefix_keys,
    prefix_values,
    out_weight,
):
    group_heads = HEADS // KVH
    score_scale = HD ** (-0.5)
    own_rows = queries.shape[0]
    owned_reqs = own_rows // DRAFT
    seq_count = lax.axis_size("seq")
    local_heads = HEADS // seq_count
    blocks = seq_count // KVH
    level_count = blocks.bit_length() - 1
    device = lax.axis_index("seq")
    head_group = device // blocks
    block_rank = device % blocks
    every_query = lax.all_gather(queries, "seq", axis=0, tiled=True)
    group_query = lax.dynamic_slice_in_dim(
        every_query, head_group * (group_heads * HD), group_heads * HD, 1
    )
    total_rows = group_query.shape[0]
    query_block = group_query.reshape(total_rows * group_heads, HD)
    key_all = prefix_keys[0]
    value_all = prefix_values[0]
    span = key_all.shape[0] // KVH
    running = None
    for part_index in range(KVH):
        key_block = key_all[part_index * span : (part_index + 1) * span]
        value_block = value_all[part_index * span : (part_index + 1) * span]
        scores = (
            lax.dot_general(
                query_block, key_block, (((1,), (1,)), ((), ())), preferred_element_type=jnp.float32
            )
            * score_scale
        )
        row_max = jnp.max(scores, axis=1)
        weights = jnp.exp(scores - row_max[:, None])
        weight_sum = jnp.sum(weights, axis=1)
        mixture = jnp.dot(
            weights.astype(jnp.bfloat16), value_block, preferred_element_type=jnp.float32
        )
        block_part = (row_max, weight_sum, mixture)
        running = block_part if running is None else merge_pair(running, block_part)
    pre_max = running[0].reshape(total_rows, group_heads)
    pre_sum = running[1].reshape(total_rows, group_heads)
    pre_out = running[2].reshape(total_rows, group_heads, HD)
    visible = tree_visible(parents)
    live_slots = jnp.arange(PRIV, dtype=jnp.int32)[None, :] < priv_lengths[:, None]
    own_maxes, own_sums, own_outs = ([], [], [])
    for group in range(KVH):
        cols_lo = group * group_heads * HD
        own_query = queries[:, cols_lo : cols_lo + group_heads * HD].reshape(
            owned_reqs, DRAFT, group_heads, HD
        )
        priv_keys = private_keys[:, :, group * HD : (group + 1) * HD]
        priv_vals = private_values[:, :, group * HD : (group + 1) * HD]
        draft_key = draft_keys[:, group * HD : (group + 1) * HD].reshape(owned_reqs, DRAFT, HD)
        draft_val = draft_values[:, group * HD : (group + 1) * HD].reshape(owned_reqs, DRAFT, HD)
        priv_scores = (
            jnp.einsum("rihd,rkd->rihk", own_query, priv_keys, preferred_element_type=jnp.float32)
            * score_scale
        )
        priv_scores = jnp.where(live_slots[:, None, None, :], priv_scores, -1e30)
        tree_scores = (
            jnp.einsum("rihd,rjd->rihj", own_query, draft_key, preferred_element_type=jnp.float32)
            * score_scale
        )
        tree_scores = jnp.where(visible[:, :, None, :], tree_scores, -1e30)
        row_max = jnp.maximum(jnp.max(priv_scores, axis=-1), jnp.max(tree_scores, axis=-1))
        priv_w = jnp.exp(priv_scores - row_max[..., None])
        tree_w = jnp.exp(tree_scores - row_max[..., None])
        weight_sum = jnp.sum(priv_w, axis=-1) + jnp.sum(tree_w, axis=-1)
        mixture = jnp.einsum(
            "rihk,rkd->rihd",
            priv_w.astype(jnp.bfloat16),
            priv_vals,
            preferred_element_type=jnp.float32,
        )
        mixture = mixture + jnp.einsum(
            "rihj,rjd->rihd",
            tree_w.astype(jnp.bfloat16),
            draft_val,
            preferred_element_type=jnp.float32,
        )
        own_maxes.append(row_max.reshape(own_rows, group_heads))
        own_sums.append(weight_sum.reshape(own_rows, group_heads))
        own_outs.append(mixture.reshape(own_rows, group_heads, HD))
    own_max = jnp.concatenate(own_maxes, axis=1)
    own_sum = jnp.concatenate(own_sums, axis=1)
    own_out = jnp.concatenate(own_outs, axis=1)
    priv_max, priv_sum, priv_out = (
        lax.all_to_all(own_max, "seq", split_axis=1, concat_axis=0, tiled=True),
        lax.all_to_all(own_sum, "seq", split_axis=1, concat_axis=0, tiled=True),
        lax.all_to_all(own_out, "seq", split_axis=1, concat_axis=0, tiled=True),
    )
    merged_parts = (pre_max, pre_sum, pre_out)
    for level in range(level_count):
        partner = from_partner((merged_parts[0], merged_parts[1], merged_parts[2]), "seq", level)
        merged_parts = merge_pair(merged_parts, partner)
    start_head = block_rank * local_heads
    peak_part = lax.dynamic_slice_in_dim(merged_parts[0], start_head, local_heads, 1)
    sum_part = lax.dynamic_slice_in_dim(merged_parts[1], start_head, local_heads, 1)
    out_part = lax.dynamic_slice_in_dim(merged_parts[2], start_head, local_heads, 1)
    joint_max = jnp.maximum(peak_part, priv_max)
    prefix_scale = jnp.exp(peak_part - joint_max)
    private_scale = jnp.exp(priv_max - joint_max)
    denom = prefix_scale * sum_part + private_scale * priv_sum
    merged = (prefix_scale[..., None] * out_part + private_scale[..., None] * priv_out) / denom[
        ..., None
    ]
    attention = merged.astype(jnp.bfloat16).reshape(total_rows, local_heads * HD)
    columns = jnp.dot(
        lax.all_gather(attention, "seq", axis=1, tiled=True),
        out_weight,
        preferred_element_type=jnp.float32,
    )
    return lax.all_to_all(columns, "seq", split_axis=0, concat_axis=1, tiled=True)


def solution(mesh):
    in_specs = (
        P(("groups", "seq"), None),
        P(("groups", "seq"), None),
        P(("groups", "seq"), None),
        P(("groups", "seq")),
        P(("groups", "seq"), None, None),
        P(("groups", "seq"), None, None),
        P(("groups", "seq")),
        P(("groups", "seq"), None, None),
        P(("groups", "seq"), None, None),
        P(None, "seq"),
    )
    out_specs = P(("groups", "seq"), None)
    return jax.shard_map(shards, mesh=mesh, in_specs=in_specs, out_specs=out_specs, check_vma=False)
```

profile of v0, /device:TPU:1, one launch (start us, length us, event | category | flops | bytes accessed | tf_op | source)
XLA Modules:
  0.0 194.9 jit_solution(10677234079913019351)
XLA Ops:
  16.9 1.2 fusion.371
  19.0 1.2 fusion.373
  30.0 7.3 %all-to-all-start = ((f32[4,16,4]{2,0,1:T(4,128)}), f32[4,16,4]{2,0,1:T(4,128)S(1)}, u32[]{:S(2)}, u32[]{:S(2)}) async-start(f32[4,16,4]{2,0,1:T(4,128)} %copy.64), calls=%async_computation | async-start | bytes 65536 | tf_op jit(solution)/shard_map/all_to_all | solution.py:141
  43.6 6.0 %all-to-all-start.2 = ((f32[4,16,4]{2,0,1:T(4,128)}), f32[4,16,4]{2,0,1:T(4,128)S(1)}, u32[]{:S(2)}, u32[]{:S(2)}) async-start(f32[4,16,4]{2,0,1:T(4,128)} %copy.88), calls=%async_computation.2 | async-start | bytes 65536 | tf_op jit(solution)/shard_map/all_to_all | solution.py:142
  50.6 5.0 %all-to-all-done.2 = f32[4,16,4]{2,0,1:T(4,128)S(1)} async-done(((f32[4,16,4]{2,0,1:T(4,128)}), f32[4,16,4]{2,0,1:T(4,128)S(1)}, u32[]{:S(2)}, u32[]{:S(2)}) %all-to-all-start.2) | async-done | bytes 1056 | tf_op jit(solution)/shard_map/all_to_all | solution.py:142
  55.6 4.1 %all-to-all-start.1 = ((f32[4,64,128]{2,0,1:T(4,128)}), f32[4,64,128]{2,0,1:T(4,128)S(1)}, u32[]{:S(2)}, u32[]{:S(2)}) async-start(f32[4,64,128]{2,0,1:T(4,128)} %copy.70), calls=%async_computation.1 | async-start | bytes 262144 | tf_op jit(solution)/shard_map/all_to_all | solution.py:143
  59.9 6.7 %all-to-all-done.1 = f32[4,64,128]{2,0,1:T(4,128)S(1)} async-done(((f32[4,64,128]{2,0,1:T(4,128)}), f32[4,64,128]{2,0,1:T(4,128)S(1)}, u32[]{:S(2)}, u32[]{:S(2)}) %all-to-all-start.1) | async-done | bytes 131104 | tf_op jit(solution)/shard_map/all_to_all | solution.py:143
  66.7 1.5 reshape.1126
  68.3 3.8 %multiply_reduce_fusion = (f32[512]{0:T(512)S(1)}, f32[512,2048]{1,0:T(8,128)}) fusion(bf16[512,128]{1,0:T(8,128)(2,1)S(1)} %reshape.1098, bf16[1,16384,128]{2,1,0:T(8,128)(2,1)} %param.17), kind=kOutput, calls=%fused_computation.8 | convolution fusion | flops 270532096 | bytes 4851712 | tf_op jit(solution)/shard_map/dot_general | solution.py:80
  72.2 2.7 %multiply_reduce_fusion.1 = (f32[512]{0:T(512)S(1)}, f32[512,2048]{1,0:T(8,128)}) fusion(bf16[512,128]{1,0:T(8,128)(2,1)S(1)} %reshape.1098, bf16[1,16384,128]{2,1,0:T(8,128)(2,1)S(1)} %copy-done.7), kind=kOutput, calls=%fused_computation.9 | convolution fusion | flops 270532096 | bytes 4851712 | tf_op jit(solution)/shard_map/dot_general | solution.py:80
  74.9 2.7 %multiply_reduce_fusion.2 = (f32[512]{0:T(512)S(1)}, f32[512,2048]{1,0:T(8,128)}) fusion(bf16[512,128]{1,0:T(8,128)(2,1)S(1)} %reshape.1098, bf16[1,16384,128]{2,1,0:T(8,128)(2,1)S(1)} %copy-done.7), kind=kOutput, calls=%fused_computation.10 | convolution fusion | flops 270532096 | bytes 4851712 | tf_op jit(solution)/shard_map/dot_general | solution.py:80
  77.5 2.7 %multiply_reduce_fusion.3 = (f32[512]{0:T(512)S(1)}, f32[512,2048]{1,0:T(8,128)}) fusion(bf16[512,128]{1,0:T(8,128)(2,1)S(1)} %reshape.1098, bf16[1,16384,128]{2,1,0:T(8,128)(2,1)S(1)} %copy-done.7), kind=kOutput, calls=%fused_computation.11 | convolution fusion | flops 270532096 | bytes 4851712 | tf_op jit(solution)/shard_map/dot_general | solution.py:80
  80.2 2.6 %multiply_reduce_fusion.4 = (f32[512]{0:T(512)S(1)}, f32[512,2048]{1,0:T(8,128)}) fusion(bf16[512,128]{1,0:T(8,128)(2,1)S(1)} %reshape.1098, bf16[1,16384,128]{2,1,0:T(8,128)(2,1)S(1)} %copy-done.7), kind=kOutput, calls=%fused_computation.12 | convolution fusion | flops 270532096 | bytes 4851712 | tf_op jit(solution)/shard_map/dot_general | solution.py:80
  82.8 2.7 %multiply_reduce_fusion.5 = (f32[512]{0:T(512)S(1)}, f32[512,2048]{1,0:T(8,128)}) fusion(bf16[512,128]{1,0:T(8,128)(2,1)S(1)} %reshape.1098, bf16[1,16384,128]{2,1,0:T(8,128)(2,1)S(1)} %copy-done.7), kind=kOutput, calls=%fused_computation.13 | convolution fusion | flops 270532096 | bytes 4851712 | tf_op jit(solution)/shard_map/dot_general | solution.py:80
  85.5 2.7 %multiply_reduce_fusion.6 = (f32[512]{0:T(512)S(1)}, f32[512,2048]{1,0:T(8,128)}) fusion(bf16[512,128]{1,0:T(8,128)(2,1)S(1)} %reshape.1098, bf16[1,16384,128]{2,1,0:T(8,128)(2,1)S(1)} %copy-done.7), kind=kOutput, calls=%fused_computation.14 | convolution fusion | flops 270532096 | bytes 4851712 | tf_op jit(solution)/shard_map/dot_general | solution.py:80
  88.2 2.7 %multiply_reduce_fusion.7 = (f32[512]{0:T(512)S(1)}, f32[512,2048]{1,0:T(8,128)}) fusion(bf16[512,128]{1,0:T(8,128)(2,1)S(1)} %reshape.1098, bf16[1,16384,128]{2,1,0:T(8,128)(2,1)S(1)} %copy-done.7), kind=kOutput, calls=%fused_computation.15 | convolution fusion | flops 270532096 | bytes 4851712 | tf_op jit(solution)/shard_map/dot_general | solution.py:80
  91.6 3.0 %fusion.14 = f32[512]{0:T(512)S(1)} fusion(f32[512,2048]{1,0:T(8,128)} %get-tuple-element.86, f32[512]{0:T(512)S(1)} %get-tuple-element.85), kind=kLoop, calls=%fused_computation.30 | loop fusion | flops 3145216 | bytes 4198400 | tf_op jit(solution)/shard_map/reduce_sum | solution.py:87
  94.8 3.0 %fusion.12 = f32[512]{0:T(512)S(1)} fusion(f32[512,2048]{1,0:T(8,128)} %get-tuple-element.88, f32[512]{0:T(512)S(1)} %get-tuple-element.87), kind=kLoop, calls=%fused_computation.28 | loop fusion | flops 3145216 | bytes 4198400 | tf_op jit(solution)/shard_map/reduce_sum | solution.py:87
  98.1 3.0 %fusion.10 = f32[512]{0:T(512)S(1)} fusion(f32[512,2048]{1,0:T(8,128)} %get-tuple-element.90, f32[512]{0:T(512)S(1)} %get-tuple-element.89), kind=kLoop, calls=%fused_computation.26 | loop fusion | flops 3145216 | bytes 4198400 | tf_op jit(solution)/shard_map/reduce_sum | solution.py:87
  101.3 3.0 %fusion.8 = f32[512]{0:T(512)S(1)} fusion(f32[512,2048]{1,0:T(8,128)} %get-tuple-element.92, f32[512]{0:T(512)S(1)} %get-tuple-element.91), kind=kLoop, calls=%fused_computation.24 | loop fusion | flops 3145216 | bytes 4198400 | tf_op jit(solution)/shard_map/reduce_sum | solution.py:87
  104.6 3.0 %fusion.6 = f32[512]{0:T(512)S(1)} fusion(f32[512,2048]{1,0:T(8,128)} %get-tuple-element.94, f32[512]{0:T(512)S(1)} %get-tuple-element.93), kind=kLoop, calls=%fused_computation.22 | loop fusion | flops 3145216 | bytes 4198400 | tf_op jit(solution)/shard_map/reduce_sum | solution.py:87
  107.8 3.0 %fusion.4 = f32[512]{0:T(512)S(1)} fusion(f32[512,2048]{1,0:T(8,128)} %get-tuple-element.96, f32[512]{0:T(512)S(1)} %get-tuple-element.95), kind=kLoop, calls=%fused_computation.20 | loop fusion | flops 3145216 | bytes 4198400 | tf_op jit(solution)/shard_map/reduce_sum | solution.py:87
  111.1 3.0 %fusion.2 = f32[512]{0:T(512)S(1)} fusion(f32[512,2048]{1,0:T(8,128)} %get-tuple-element.84, f32[512]{0:T(512)S(1)} %get-tuple-element.83), kind=kLoop, calls=%fused_computation.18 | loop fusion | flops 3145216 | bytes 4198400 | tf_op jit(solution)/shard_map/reduce_sum | solution.py:87
  114.3 3.2 %fusion = f32[512]{0:T(512)S(1)} fusion(f32[512,2048]{1,0:T(8,128)} %get-tuple-element.98, f32[512]{0:T(512)S(1)} %get-tuple-element.97), kind=kLoop, calls=%fused_computation.16 | loop fusion | flops 3145216 | bytes 4198400 | tf_op jit(solution)/shard_map/reduce_sum | solution.py:87
  117.8 1.2 collective-permute-start.2
  119.2 3.3 %fusion.54 = f32[512,128]{1,0:T(8,128)S(1)} fusion(f32[512,2048]{1,0:T(8,128)} %get-tuple-element.84, f32[512]{0:T(512)S(1)} %get-tuple-element.83, bf16[1,16384,128]{2,1,0:T(8,128)(2,1)} %param.18, f32[512]{0:T(512)S(1)} %get-tuple-element.49), kind=kOutput, calls=%fused_computation.58 | convolution fusion | flops 271646720 | bytes 4984832 | tf_op jit(solution)/shard_map/dot_general | solution.py:88
  122.5 2.0 %fusion.111 = f32[512,128]{1,0:T(8,128)S(1)} fusion(f32[512,128]{1,0:T(8,128)S(1)} %fusion.54, f32[512,2048]{1,0:T(8,128)S(1)} %copy-done.6, f32[512]{0:T(512)S(1)} %get-tuple-element.97, bf16[1,16384,128]{2,1,0:T(8,128)(2,1)} %param.18, f32[512]{0:T(512)S(1)} %get-tuple-element.50, f32[512]{0:T(512)S(1)} %get-tuple-element.46), kind=kOutput, calls=%fused_computation.77 | convolution fusion | flops 271777792 | bytes 5249024 | tf_op jit(solution)/shard_map/dot_general | solution.py:88
  124.6 2.0 %fusion.108 = f32[512,128]{1,0:T(8,128)S(1)} fusion(f32[512,128]{1,0:T(8,128)S(1)} %fusion.111, f32[512,2048]{1,0:T(8,128)S(1)} %copy-done.5, f32[512]{0:T(512)S(1)} %get-tuple-element.95, bf16[1,16384,128]{2,1,0:T(8,128)(2,1)} %param.18, f32[512]{0:T(512)S(1)} %get-tuple-element.47, f32[512]{0:T(512)S(1)} %get-tuple-element.48), kind=kOutput, calls=%fused_computation.76 | convolution fusion | flops 271777792 | bytes 5249024 | tf_op jit(solution)/shard_map/dot_general | solution.py:88
  126.6 2.4 %fusion.105 = f32[512,128]{1,0:T(8,128)S(1)} fusion(f32[512,128]{1,0:T(8,128)S(1)} %fusion.108, f32[512,2048]{1,0:T(8,128)S(1)} %copy-done.4, f32[512]{0:T(512)S(1)} %get-tuple-element.93, bf16[1,16384,128]{2,1,0:T(8,128)(2,1)} %param.18, f32[512]{0:T(512)S(1)} %get-tuple-element.45, f32[512]{0:T(512)S(1)} %get-tuple-element.42), kind=kOutput, calls=%fused_computation.75 | convolution fusion | flops 271777792 | bytes 5249024 | tf_op jit(solution)/shard_map/dot_general | solution.py:88
  136.3 34.7 %all-gather.4.cloned.1.call-done = bf16[64,8192]{1,0:T(8,128)(2,1)} async-done(((bf16[64,512]{1,0:T(8,128)(2,1)}), bf16[64,8192]{1,0:T(8,128)(2,1)}) %all-gather.4.cloned.1.call-update) | async-done | bytes 1048592 | tf_op jit(solution)/shard_map/all_gather | solution.py:162
  171.1 5.3 %fusion.385 = f32[64,512]{1,0:T(8,128)S(1)} fusion(bf16[64,8192]{1,0:T(8,128)(2,1)} %all-gather.4.cloned.1.call-done, bf16[8192,512]{1,0:T(8,128)(2,1)} %param.19), kind=kOutput, calls=%fused_computation.421 | convolution fusion | flops 536870912 | bytes 9568256 | tf_op jit(solution)/shard_map/dot_general | solution.py:161
  176.4 11.0 %all_to_all.69 = f32[16,4,512]{2,1,0:T(4,128)S(1)} all-to-all(f32[16,4,512]{2,1,0:T(4,128)S(1)} %all_to_all.61), channel_id=1, replica_groups=mesh['groups'=2,'seq'=16] {'seq'}, dimensions={0} | all-to-all | bytes 262144 | tf_op jit(solution)/shard_map/all_to_all | solution.py:166
  (180 shorter events, 38.2 us)
Async XLA Ops:
  6.5 31.0 %copy-start.9 = (bf16[1,1024,1024]{2,1,0:T(8,128)(2,1)S(1)}, bf16[1,1024,1024]{2,1,0:T(8,128)(2,1)}, u32[]{:S(2)}) copy-start(bf16[1,1024,1024]{2,1,0:T(8,128)(2,1)} %param.15) | copy-start | bytes 6291460
  6.5 33.6 %copy-start.10 = (bf16[4,1024]{1,0:T(4,128)(2,1)S(1)}, bf16[4,1024]{1,0:T(4,128)(2,1)}, u32[]{:S(2)}) copy-start(bf16[4,1024]{1,0:T(4,128)(2,1)} %param.12) | copy-start | bytes 24580
  6.5 60.2 %all-gather.6.cloned.1.call-start = ((), (), s32[]{:S(2)}) async-start(), calls=%async_computation.5 | async-start | bytes 1114112 | tf_op jit(solution)/shard_map/all_gather | solution.py:66
  30.0 13.7 %all-to-all-start = ((f32[4,16,4]{2,0,1:T(4,128)}), f32[4,16,4]{2,0,1:T(4,128)S(1)}, u32[]{:S(2)}, u32[]{:S(2)}) async-start(f32[4,16,4]{2,0,1:T(4,128)} %copy.64), calls=%async_computation | async-start | bytes 65536 | tf_op jit(solution)/shard_map/all_to_all | solution.py:141
  43.6 11.9 %all-to-all-start.2 = ((f32[4,16,4]{2,0,1:T(4,128)}), f32[4,16,4]{2,0,1:T(4,128)S(1)}, u32[]{:S(2)}, u32[]{:S(2)}) async-start(f32[4,16,4]{2,0,1:T(4,128)} %copy.88), calls=%async_computation.2 | async-start | bytes 65536 | tf_op jit(solution)/shard_map/all_to_all | solution.py:142
  55.6 11.1 %all-to-all-start.1 = ((f32[4,64,128]{2,0,1:T(4,128)}), f32[4,64,128]{2,0,1:T(4,128)S(1)}, u32[]{:S(2)}, u32[]{:S(2)}) async-start(f32[4,64,128]{2,0,1:T(4,128)} %copy.70), calls=%async_computation.1 | async-start | bytes 262144 | tf_op jit(solution)/shard_map/all_to_all | solution.py:143
  59.7 111.4 %all-gather.4.cloned.1.call-start = ((), (), s32[]{:S(2)}) async-start(), calls=%async_computation.4 | async-start | bytes 1114112 | tf_op jit(solution)/shard_map/all_gather | solution.py:162
  68.3 3.8 %copy-start.7 = (bf16[1,16384,128]{2,1,0:T(8,128)(2,1)S(1)}, bf16[1,16384,128]{2,1,0:T(8,128)(2,1)}, u32[]{:S(2)}) copy-start(bf16[1,16384,128]{2,1,0:T(8,128)(2,1)} %param.17) | copy-start | bytes 12582916
  117.8 4.7 %copy-start.6 = (f32[512,2048]{1,0:T(8,128)S(1)}, f32[512,2048]{1,0:T(8,128)}, u32[]{:S(2)}) copy-start(f32[512,2048]{1,0:T(8,128)} %get-tuple-element.98) | copy-start | bytes 12582916
  117.8 16.2 %collective-permute-start.2 = (f32[64,8]{0,1:T(8,128)S(1)}, f32[64,8]{0,1:T(8,128)S(1)}, u32[]{:S(2)}, u32[]{:S(2)}) collective-permute-start(f32[64,8]{0,1:T(8,128)S(1)} %get-tuple-element.12), channel_id=1, source_target_pairs={{0,1},{1,0},{2,3},{3,2},{4,5},{5,4},{6,7},{7,6},{8,9},{9,8},{10,11... | collective-permute-start | bytes 6152 | tf_op jit(solution)/shard_map/ppermute | solution.py:14
  119.1 15.0 %collective-permute-start = (f32[64,8]{0,1:T(8,128)S(1)}, f32[64,8]{0,1:T(8,128)S(1)}, u32[]{:S(2)}, u32[]{:S(2)}) collective-permute-start(f32[64,8]{0,1:T(8,128)S(1)} %get-tuple-element.13), channel_id=1, source_target_pairs={{0,1},{1,0},{2,3},{3,2},{4,5},{5,4},{6,7},{7,6},{8,9},{9,8},{10,11... | collective-permute-start | bytes 6152 | tf_op jit(solution)/shard_map/ppermute | solution.py:14
  119.2 5.4 %copy-start.5 = (f32[512,2048]{1,0:T(8,128)S(1)}, f32[512,2048]{1,0:T(8,128)}, u32[]{:S(2)}) copy-start(f32[512,2048]{1,0:T(8,128)} %get-tuple-element.96) | copy-start | bytes 12582916
  122.5 4.1 %copy-start.4 = (f32[512,2048]{1,0:T(8,128)S(1)}, f32[512,2048]{1,0:T(8,128)}, u32[]{:S(2)}) copy-start(f32[512,2048]{1,0:T(8,128)} %get-tuple-element.94) | copy-start | bytes 12582916
  124.5 4.5 %copy-start.3 = (f32[512,2048]{1,0:T(8,128)S(1)}, f32[512,2048]{1,0:T(8,128)}, u32[]{:S(2)}) copy-start(f32[512,2048]{1,0:T(8,128)} %get-tuple-element.92) | copy-start | bytes 12582916
  124.6 4.5 %copy-start.8 = (bf16[1,16384,128]{2,1,0:T(8,128)(2,1)S(1)}, bf16[1,16384,128]{2,1,0:T(8,128)(2,1)}, u32[]{:S(2)}) copy-start(bf16[1,16384,128]{2,1,0:T(8,128)(2,1)} %param.18) | copy-start | bytes 12582916
  126.6 3.3 %copy-start.2 = (f32[512,2048]{1,0:T(8,128)S(1)}, f32[512,2048]{1,0:T(8,128)}, u32[]{:S(2)}) copy-start(f32[512,2048]{1,0:T(8,128)} %get-tuple-element.90) | copy-start | bytes 12582916
  129.0 2.4 %copy-start.1 = (f32[512,2048]{1,0:T(8,128)S(1)}, f32[512,2048]{1,0:T(8,128)}, u32[]{:S(2)}) copy-start(f32[512,2048]{1,0:T(8,128)} %get-tuple-element.88) | copy-start | bytes 12582916
  129.9 2.7 %copy-start = (f32[512,2048]{1,0:T(8,128)S(1)}, f32[512,2048]{1,0:T(8,128)}, u32[]{:S(2)}) copy-start(f32[512,2048]{1,0:T(8,128)} %get-tuple-element.86) | copy-start | bytes 12582916
  133.4 1.8 collective-permute-start.1
Sparse Core Ops, SparseCore 0:
  9.5 41.0 all-gather.5
  136.4 34.5 all-gather.3
where the time goes:
time: 197 us; the launch traced here: 195 us
  matrix products  60.9 us (31%)
  waiting for transfers between devices  47.8 us (24%)
  other arithmetic  29.8 us (15%)
  starting transfers between devices  19.5 us (10%)
  between operations  14.6 us (7%)
  local copies, waits for them, and re-layouts  11.3 us (6%)
  blocking collectives  11 us (6%)
    all_gather x1, waiting for transfers between devices, shards(): lax.all_gather(attention, 'seq', axis=1, tiled=True)  34.7 us
    reduce_sum x8, other arithmetic, shards(): weight_sum = jnp.sum(weights, axis=1)  24.4 us
    dot_general x8, matrix products, shards(): lax.dot_general(query_block, key_block, (((1,), (1,)), ((), ())), preferr...  22.5 us
    dot_general x8, matrix products, shards(): jnp.dot(weights.astype(jnp.bfloat16), value_block, preferred_element_type...  13.1 us
    all_to_all x1, blocking collectives, shards(): lax.all_to_all(columns, 'seq', split_axis=0, concat_axis=1, tiled=True)  11 us
    dot_general x8, matrix products, shards(): jnp.einsum('rihd,rkd->rihk', own_query, priv_keys, preferred_element_type...  9.86 us
    all_to_all x1, starting transfers between devices, shards(): lax.all_to_all(own_max, 'seq', split_axis=1, concat_axis=0, tiled=True)  7.35 us
    dot_general x8, matrix products, shards(): jnp.einsum('rihd,rjd->rihj', own_query, draft_key, preferred_element_type...  6.76 us
  transfers between devices with their start and end apart: 8, of which 4 were waited for; matrix products, arithmetic and copies ran while one was open for 22% of the time, Pallas kernels for 0%

commit v1 on v0

v1 whole, which is shorter than its diff:
```python
import functools
import math

import jax
import jax.numpy as jnp
from jax import lax
from jax.experimental import pallas as pl
from jax.experimental.pallas import tpu as pltpu
from jax.sharding import PartitionSpec as P

HEADS = 64
KVH = 8
HD = 128
GH = HEADS // KVH
MESH = pl.DeviceIdType.MESH
F32 = jnp.float32
BF16 = jnp.bfloat16


def kernel(
    n,
    q_ref,
    dk_ref,
    dv_ref,
    par_ref,
    len_ref,
    pk_hbm,
    pv_hbm,
    k_hbm,
    v_hbm,
    w_hbm,
    o_ref,
    pk,
    pv,
    k,
    v,
    w,
    qf,
    qs,
    qbuf,
    dk_pad,
    dv_pad,
    priv_send,
    priv_buf,
    m_scr,
    part,
    merge_buf,
    fin,
    att,
    gat,
    acc,
    col,
    load_sem,
    q_ssem,
    q_rsem,
    p_ssem,
    p_rsem,
    m_ssem,
    m_rsem,
    g_ssem,
    g_rsem,
    o_ssem,
    o_rsem,
):
    me = lax.axis_index("seq")
    blocks = n // KVH
    lh = HEADS // n
    draft = q_ref.shape[0]
    gr = GH * draft
    lr = lh * draft
    lc = lh * HD
    cols = w.shape[1]
    g_me = me // blocks
    b_me = me % blocks
    c2 = HD**-0.5 * math.log2(math.e)

    loads = [
        pltpu.make_async_copy(pk_hbm.at[0], pk, load_sem.at[0]),
        pltpu.make_async_copy(pv_hbm.at[0], pv, load_sem.at[1]),
        pltpu.make_async_copy(k_hbm.at[0], k, load_sem.at[2]),
        pltpu.make_async_copy(v_hbm.at[0], v.at[:, pl.ds(0, HD)], load_sem.at[3]),
        pltpu.make_async_copy(w_hbm, w, load_sem.at[4]),
    ]
    for load in loads:
        load.start()

    def remote(src, dst, ssem, rsem, to):
        return pltpu.make_async_remote_copy(
            src_ref=src, dst_ref=dst, send_sem=ssem, recv_sem=rsem,
            device_id={"seq": to}, device_id_type=MESH,
        )

    barrier = pltpu.get_barrier_semaphore()
    for off in range(1, n):
        pl.semaphore_signal(
            barrier, inc=1, device_id={"seq": lax.rem(me + off, n)}, device_id_type=MESH
        )
    for g in range(KVH):
        for h in range(GH):
            at = (g * GH + h) * HD
            qf[g, h * draft : (h + 1) * draft, :] = q_ref[:, at : at + HD].astype(F32)
        qs[g] = qf[g].astype(BF16)
    dk_pad[...] = jnp.zeros_like(dk_pad)
    dv_pad[...] = jnp.zeros_like(dv_pad)
    dk_pad[0:draft, :] = dk_ref[...].astype(F32)
    dv_pad[0:draft, :] = dv_ref[...].astype(F32)
    qbuf[me] = qs[g_me]
    pl.semaphore_wait(barrier, n - 1)

    q_sends = []
    for off in range(1, n):
        to = lax.rem(me + off, n)
        q_sends.append(
            remote(qs.at[to // blocks], qbuf.at[me], q_ssem.at[off], q_rsem.at[me], to)
        )
        q_sends[-1].start()

    v[:, HD:] = jnp.ones((v.shape[0], HD), BF16)

    pad = dk_pad.shape[0]
    row_i = lax.broadcasted_iota(jnp.int32, (gr, pad), 0) % draft
    col_j = lax.broadcasted_iota(jnp.int32, (gr, pad), 1)
    seen = [[None] * draft for _ in range(draft)]
    visible = (row_i == col_j).astype(jnp.int32)
    for i in range(draft):
        for j in range(i):
            hit = (par_ref[i] == j).astype(jnp.int32)
            for mid in range(j + 1, i):
                hit = hit + (par_ref[i] == mid).astype(jnp.int32) * seen[mid][j]
            seen[i][j] = hit
            visible = jnp.where((row_i == i) & (col_j == j), hit, visible)
    slots = pk.shape[0]
    live = lax.broadcasted_iota(jnp.int32, (gr, slots), 1) < len_ref[0]
    lane = lax.broadcasted_iota(jnp.int32, (gr, HD), 1)
    loads[0].wait()
    loads[1].wait()
    nt = (((1,), (1,)), ((), ()))
    for g in range(KVH):
        cs = slice(g * HD, (g + 1) * HD)
        qg = qs[g]
        s = lax.dot_general(qg, pk[:, cs], nt, preferred_element_type=F32)
        t = lax.dot_general(qg, dk_pad[:, cs].astype(BF16), nt, preferred_element_type=F32)
        s = jnp.where(live, s, -1e30)
        t = jnp.where(visible > 0, t, -1e30)
        mx = jnp.maximum(
            jnp.max(s, axis=1, keepdims=True), jnp.max(t, axis=1, keepdims=True)
        )
        ps = jnp.exp2((s - mx) * c2)
        pt = jnp.exp2((t - mx) * c2)
        sm = jnp.sum(ps, axis=1, keepdims=True) + jnp.sum(pt, axis=1, keepdims=True)
        mix = jnp.dot(ps.astype(BF16), pv[:, cs], preferred_element_type=F32)
        mix = mix + jnp.dot(
            pt.astype(BF16), dv_pad[:, cs].astype(BF16), preferred_element_type=F32
        )
        priv_send[g, :, 0:HD] = mix
        priv_send[g, :, HD:] = jnp.where(lane == 0, mx, sm)

    def own_rows(b):
        return pl.ds(pl.multiple_of(b * lr, lr), lr)

    p_sends = []
    for off in range(1, n):
        to = lax.rem(me + off, n)
        p_sends.append(
            remote(
                priv_send.at[to // blocks, own_rows(to % blocks)], priv_buf.at[me],
                p_ssem.at[off], p_rsem.at[me], to,
            )
        )
        p_sends[-1].start()
    priv_buf[me] = priv_send[g_me, own_rows(b_me), :]

    for off in range(1, n):
        src = lax.rem(me + off, n)
        remote(qs.at[0], qbuf.at[src], q_ssem.at[off], q_rsem.at[src], src).wait_recv()
    loads[2].wait()
    loads[3].wait()
    rows = n * gr
    rb = 256
    ch = 2048
    reqs = rb // gr
    m_scr[...] = jnp.full_like(m_scr, -1e30)
    part[...] = jnp.zeros_like(part)

    def chunk(j, _):
        ks = pl.ds(pl.multiple_of(j * ch, ch), ch)
        kb = k[ks, :]
        vb = v[ks, :]
        for r in range(rows // rb):
            rs = slice(r * rb, (r + 1) * rb)
            qr = qbuf[r * reqs : (r + 1) * reqs].reshape(rb, HD)
            s = lax.dot_general(qr, kb, nt, preferred_element_type=F32)
            old = m_scr[rs, :]
            new = jnp.maximum(old, jnp.max(s, axis=1, keepdims=True))
            m_scr[rs, :] = new
            p = jnp.exp2((s - new[:, 0:1]) * c2).astype(BF16)
            fac = jnp.exp2((old - new) * c2)[:, 0:1]
            mix = jnp.dot(p, vb, preferred_element_type=F32)
            was = part[r * reqs : (r + 1) * reqs].reshape(rb, 2 * HD)
            part[r * reqs : (r + 1) * reqs] = (was * fac + mix).reshape(reqs, gr, 2 * HD)
        return 0

    lax.fori_loop(0, k.shape[0] // ch, chunk, 0)
    lane_m = lax.broadcasted_iota(jnp.int32, (n, gr, HD), 2)
    part[:, :, HD:] = jnp.where(lane_m == 0, m_scr[...].reshape(n, gr, HD), part[:, :, HD:])

    m_sends = []
    for off in range(1, blocks):
        b_to = lax.rem(b_me + off, blocks)
        m_sends.append(
            remote(
                part.at[:, own_rows(b_to)], merge_buf.at[b_me],
                m_ssem.at[off], m_rsem.at[b_me], g_me * blocks + b_to,
            )
        )
        m_sends[-1].start()
    for off in range(1, n):
        src = lax.rem(me + off, n)
        remote(
            priv_send.at[0, own_rows(0)], priv_buf.at[src], p_ssem.at[off], p_rsem.at[src], src
        ).wait_recv()
    pieces = [priv_buf[...], part[:, own_rows(b_me), :]]
    for off in range(1, blocks):
        b_src = lax.rem(b_me + off, blocks)
        remote(
            part.at[:, own_rows(0)], merge_buf.at[b_src],
            m_ssem.at[off], m_rsem.at[b_src], g_me * blocks + b_src,
        ).wait_recv()
        pieces.append(merge_buf[b_src])
    pieces = [x.reshape(n * lr, 2 * HD) for x in pieces]
    peak = functools.reduce(jnp.maximum, [x[:, HD : HD + 1] for x in pieces])
    facs = [jnp.exp2((x[:, HD : HD + 1] - peak) * c2) for x in pieces]
    den = sum(f * x[:, HD + 1 : HD + 2] for f, x in zip(facs, pieces))
    num = sum(f * x[:, 0:HD] for f, x in zip(facs, pieces))
    fin[...] = (num / den).reshape(n, lr, HD)
    for r in range(n):
        for h in range(lh):
            att[r * draft : (r + 1) * draft, h * HD : (h + 1) * HD] = fin[
                r, h * draft : (h + 1) * draft, :
            ]
    gat[me] = att[...].astype(BF16)

    core = me % 2
    chip = me // 2
    line = chip // 2
    side = chip % 2
    lines = n // 4

    def dev(line_at, side_at, core_at):
        return (line_at * 2 + side_at) * 2 + core_at

    g_sends = []

    def forward(src, to):
        g_sends.append(
            remote(gat.at[src], gat.at[src], g_ssem.at[len(g_sends)], g_rsem.at[src], to)
        )
        g_sends[-1].start()

    def arrived(src):
        remote(gat.at[src], gat.at[src], g_ssem.at[0], g_rsem.at[src], me ^ 1).wait_recv()

    def project(src):
        ws = pl.ds(pl.multiple_of(src * lc, lc), lc)
        return jnp.dot(gat[src], w[ws, :], preferred_element_type=F32)

    across = dev(line, 1 - side, core)
    partner = dev(line, side, 1 - core)
    forward(me, across)
    for off in range(1, lines):
        forward(me, dev(lax.rem(line + off, lines), side, core))
    forward(me, partner)
    loads[4].wait()
    acc[...] = project(me)
    for off in range(1, lines):
        src = dev(lax.rem(line + off, lines), side, core)
        arrived(src)
        forward(src, across)
        forward(src, partner)
        acc[...] += project(src)
    for off in range(lines):
        src = dev(lax.rem(line + off, lines), 1 - side, core)
        arrived(src)
        forward(src, partner)
        acc[...] += project(src)
    for side_at in (side, 1 - side):
        for off in range(lines):
            src = dev(lax.rem(line + off, lines), side_at, 1 - core)
            arrived(src)
            acc[...] += project(src)
    for r in range(n):
        col[r] = acc[r * draft : (r + 1) * draft, :]

    def out_cols(src):
        return o_ref.at[:, pl.ds(pl.multiple_of(src * cols, cols), cols)]

    o_sends = []
    for off in range(1, n):
        to = lax.rem(me + off, n)
        o_sends.append(
            remote(col.at[to], out_cols(me), o_ssem.at[off], o_rsem.at[me], to)
        )
        o_sends[-1].start()
    o_ref[:, pl.ds(pl.multiple_of(me * cols, cols), cols)] = col[me]
    for off in range(1, n):
        src = lax.rem(me + off, n)
        remote(col.at[0], out_cols(src), o_ssem.at[off], o_rsem.at[src], src).wait_recv()
    for sends in (q_sends, p_sends, m_sends, g_sends, o_sends):
        for send in sends:
            send.wait_send()


def shards(
    n, queries, draft_keys, draft_values, parents, private_keys, private_values,
    priv_lengths, prefix_keys, prefix_values, out_weight,
):
    blocks = n // KVH
    lh = HEADS // n
    draft = queries.shape[0]
    gr = GH * draft
    lr = lh * draft
    slots = private_keys.shape[1]
    span = prefix_keys.shape[1]
    d, cols = out_weight.shape
    vm = pl.BlockSpec(memory_space=pltpu.VMEM)
    sm = pl.BlockSpec(memory_space=pltpu.SMEM)
    hb = pl.BlockSpec(memory_space=pl.ANY)
    dma = pltpu.SemaphoreType.DMA
    return pl.pallas_call(
        functools.partial(kernel, n),
        out_shape=jax.ShapeDtypeStruct((draft, n * cols), F32),
        in_specs=[vm, vm, vm, sm, sm, hb, hb, hb, hb, hb],
        out_specs=vm,
        scratch_shapes=[
            pltpu.VMEM((slots, KVH * HD), BF16),
            pltpu.VMEM((slots, KVH * HD), BF16),
            pltpu.VMEM((span, HD), BF16),
            pltpu.VMEM((span, 2 * HD), BF16),
            pltpu.VMEM((d, cols), BF16),
            pltpu.VMEM((KVH, gr, HD), F32),
            pltpu.VMEM((KVH, gr, HD), BF16),
            pltpu.VMEM((n, gr, HD), BF16),
            pltpu.VMEM((16, KVH * HD), F32),
            pltpu.VMEM((16, KVH * HD), F32),
            pltpu.VMEM((KVH, gr, 2 * HD), F32),
            pltpu.VMEM((n, lr, 2 * HD), F32),
            pltpu.VMEM((n * gr, HD), F32),
            pltpu.VMEM((n, gr, 2 * HD), F32),
            pltpu.VMEM((blocks, n, lr, 2 * HD), F32),
            pltpu.VMEM((n, lr, HD), F32),
            pltpu.VMEM((n * draft, lh * HD), F32),
            pltpu.VMEM((n, n * draft, lh * HD), BF16),
            pltpu.VMEM((n * draft, cols), F32),
            pltpu.VMEM((n, draft, cols), F32),
            dma((5,)),
            dma((n,)), dma((n,)), dma((n,)), dma((n,)),
            dma((blocks,)), dma((blocks,)),
            dma((n,)), dma((n,)), dma((n,)), dma((n,)),
        ],
        compiler_params=pltpu.CompilerParams(
            collective_id=0, has_side_effects=True, vmem_limit_bytes=58 << 20
        ),
        cost_estimate=pl.CostEstimate(
            flops=4 * n * gr * span * HD, bytes_accessed=24 << 20, transcendentals=n * gr * span
        ),
    )(
        queries, draft_keys, draft_values, parents, priv_lengths,
        private_keys, private_values, prefix_keys, prefix_values, out_weight,
    )


def solution(mesh):
    both = ("groups", "seq")
    in_specs = (
        P(both, None), P(both, None), P(both, None), P(both),
        P(both, None, None), P(both, None, None), P(both),
        P(both, None, None), P(both, None, None), P(None, "seq"),
    )
    return jax.shard_map(
        functools.partial(shards, mesh.shape["seq"]),
        mesh=mesh, in_specs=in_specs, out_specs=P(both, None), check_vma=False,
    )
```

time: 197 us -> 53.4 us (0.27)
  matrix products: 60.9 us -> 0 us
  Pallas kernels: 0 us -> 50.7 us
  waiting for transfers between devices: 47.8 us -> 0 us
  other arithmetic: 29.8 us -> 0 us
  starting transfers between devices: 19.5 us -> 0 us
  between operations: 14.6 us -> 0.66 us
  blocking collectives: 11 us -> 0 us
  local copies, waits for them, and re-layouts: 11.3 us -> 1.57 us
    dot_general x49 -> x0, matrix products: 60.9 us -> none  [the longest x8 22.5 us: shards(): lax.dot_general(query_block, key_block, (((1,), (1,)), ((), ())), preferr...]
    pallas_call x0 -> x1, Pallas kernels: none -> 50.7 us  [shards(): pl.pallas_call(functools.partial(kernel, n), out_shape=jax.ShapeDtypeStru...]
    all_gather x2 -> x0, waiting for transfers between devices: 34.8 us -> none  [the longest x1 34.7 us: shards(): lax.all_gather(attention, 'seq', axis=1, tiled=True)]
    reduce_sum x26 -> x0, other arithmetic: 27.8 us -> none  [the longest x8 24.4 us: shards(): weight_sum = jnp.sum(weights, axis=1)]
    all_to_all x3 -> x0, starting transfers between devices: 17.5 us -> none  [the longest x1 7.35 us: shards(): lax.all_to_all(own_max, 'seq', split_axis=1, concat_axis=0, tiled=True)]
    all_to_all x3 -> x0, waiting for transfers between devices: 11.7 us -> none  [the longest x1 6.74 us: shards(): lax.all_to_all(own_out, 'seq', split_axis=1, concat_axis=0, tiled=True)]
    all_to_all x1 -> x0, blocking collectives: 11 us -> none  [shards(): lax.all_to_all(columns, 'seq', split_axis=0, concat_axis=1, tiled=True)]
    unnamed x26 -> x1, local copies, waits for them, and re-layouts: 4.69 us -> 1.57 us
  transfers between devices with their start and end apart: 8 -> 0, of which waited for: 4 -> 0; matrix products, arithmetic and copies ran while one was open for 22% -> 0% of each run, Pallas kernels for 0% -> 0%
where the time goes in v1:
time: 53.4 us; the launch traced here: 52.9 us
  Pallas kernels  50.7 us (95%)
  local copies, waits for them, and re-layouts  1.57 us (3%)
  between operations  0.66 us (1%)
    pallas_call x1, Pallas kernels, shards(): pl.pallas_call(functools.partial(kernel, n), out_shape=jax.ShapeDtypeStru...  50.7 us
    unnamed x1, local copies, waits for them, and re-layouts  1.57 us

profile of v1, /device:TPU:1, one launch (start us, length us, event | category | flops | bytes accessed | tf_op | source)
XLA Modules:
  0.0 52.9 jit_solution(9102513315475783008)
XLA Ops:
  0.7 50.7 %shard_map.100 = f32[4,8192]{1,0:T(4,128)} custom-call(bf16[4,8192]{1,0:T(4,128)(2,1)} %q_ref.1, bf16[4,1024]{1,0:T(4,128)(2,1)} %dk_ref.1, bf16[4,1024]{1,0:T(4,128)(2,1)} %dv_ref.1, s32[4]{0:T(128)} %par_ref.1, s32[1]{0:T(128)S(6)} %copy.12.len_ref, bf16[1,1024,1024]{2,1,0:T(8,128)(2,1)} %pk_hbm.1, bf16[1,1024,1024]{2,1,0:T(8,128)(2,1)} %pv_hbm.1, ...), custom_call_target="tpu_custom_call" | custom-call | flops 4294967296 | bytes 25165824 | tf_op jit(solution)/shard_map/pallas_call | solution.py:329
  51.3 1.6 %copy.13 = f32[4,8192]{1,0:T(4,128)} copy(f32[4,8192]{1,0:T(4,128)} %shard_map.100) | data formatting | bytes 262144

commit v2 on v1

v2 whole, which is shorter than its diff:
```python
import functools
import math

import jax
import jax.numpy as jnp
from jax import lax
from jax.experimental import pallas as pl
from jax.experimental.pallas import tpu as pltpu
from jax.sharding import PartitionSpec as P

HEADS = 64
KVH = 8
HD = 128
GH = HEADS // KVH
PARTS = 2
MESH = pl.DeviceIdType.MESH
F32 = jnp.float32
BF16 = jnp.bfloat16


def kernel(
    n,
    q_ref,
    dk_ref,
    dv_ref,
    par_ref,
    len_ref,
    pk_hbm,
    pv_hbm,
    k_hbm,
    v_hbm,
    w_hbm,
    o_ref,
    pk,
    pv,
    k,
    v,
    w,
    qf,
    qs,
    qbuf,
    dk_pad,
    dv_pad,
    priv_send,
    priv_buf,
    part,
    merge_buf,
    fin,
    att,
    gat,
    col_f,
    col,
    obuf,
    load_sem,
    q_ssem,
    q_rsem,
    p_ssem,
    p_rsem,
    m_ssem,
    m_rsem,
    g_ssem,
    g_rsem,
    o_ssem,
    o_rsem,
):
    me = lax.axis_index("seq")
    blocks = n // KVH
    lh = HEADS // n
    draft = q_ref.shape[0]
    gr = GH * draft
    lr = lh * draft
    lc = lh * HD
    cols = w.shape[1]
    g_me = me // blocks
    b_me = me % blocks
    rp = n // PARTS
    c2 = HD**-0.5 * math.log2(math.e)

    loads = [
        pltpu.make_async_copy(pk_hbm.at[0], pk, load_sem.at[0]),
        pltpu.make_async_copy(pv_hbm.at[0], pv, load_sem.at[1]),
        pltpu.make_async_copy(k_hbm.at[0], k, load_sem.at[2]),
        pltpu.make_async_copy(v_hbm.at[0], v.at[:, pl.ds(0, HD)], load_sem.at[3]),
        pltpu.make_async_copy(w_hbm, w, load_sem.at[4]),
    ]
    for load in loads[:4]:
        load.start()

    def pos(r):
        return r % PARTS * rp + r // PARTS

    here = pos(me)

    def remote(src, dst, ssem, rsem, to):
        return pltpu.make_async_remote_copy(
            src_ref=src, dst_ref=dst, send_sem=ssem, recv_sem=rsem,
            device_id={"seq": to}, device_id_type=MESH,
        )

    barrier = pltpu.get_barrier_semaphore()
    for off in range(1, n):
        pl.semaphore_signal(
            barrier, inc=1, device_id={"seq": lax.rem(me + off, n)}, device_id_type=MESH
        )
    for g in range(KVH):
        for h in range(GH):
            at = (g * GH + h) * HD
            qf[g, h * draft : (h + 1) * draft, :] = q_ref[:, at : at + HD].astype(F32)
        qs[g] = qf[g].astype(BF16)
    dk_pad[...] = jnp.zeros_like(dk_pad)
    dv_pad[...] = jnp.zeros_like(dv_pad)
    dk_pad[0:draft, :] = dk_ref[...].astype(F32)
    dv_pad[0:draft, :] = dv_ref[...].astype(F32)
    qbuf[here] = qs[g_me]
    pl.semaphore_wait(barrier, n - 1)

    q_sends = []
    for off in range(1, n):
        to = lax.rem(me + off, n)
        q_sends.append(
            remote(qs.at[to // blocks], qbuf.at[here], q_ssem.at[off], q_rsem.at[me], to)
        )
        q_sends[-1].start()
    loads[4].start()

    v[:, HD:] = jnp.ones((v.shape[0], HD), BF16)

    pad = dk_pad.shape[0]
    row_i = lax.broadcasted_iota(jnp.int32, (gr, pad), 0) % draft
    col_j = lax.broadcasted_iota(jnp.int32, (gr, pad), 1)
    seen = [[None] * draft for _ in range(draft)]
    visible = (row_i == col_j).astype(jnp.int32)
    for i in range(draft):
        for j in range(i):
            hit = (par_ref[i] == j).astype(jnp.int32)
            for mid in range(j + 1, i):
                hit = hit + (par_ref[i] == mid).astype(jnp.int32) * seen[mid][j]
            seen[i][j] = hit
            visible = jnp.where((row_i == i) & (col_j == j), hit, visible)
    slots = pk.shape[0]
    live = lax.broadcasted_iota(jnp.int32, (gr, slots), 1) < len_ref[0]
    lane = lax.broadcasted_iota(jnp.int32, (gr, HD), 1)
    loads[0].wait()
    loads[1].wait()
    nt = (((1,), (1,)), ((), ()))
    for g in range(KVH):
        cs = slice(g * HD, (g + 1) * HD)
        qg = qs[g]
        s = lax.dot_general(qg, pk[:, cs], nt, preferred_element_type=F32)
        t = lax.dot_general(qg, dk_pad[:, cs].astype(BF16), nt, preferred_element_type=F32)
        s = jnp.where(live, s, -1e30)
        t = jnp.where(visible > 0, t, -1e30)
        mx = jnp.maximum(
            jnp.max(s, axis=1, keepdims=True), jnp.max(t, axis=1, keepdims=True)
        )
        ps = jnp.exp2((s - mx) * c2)
        pt = jnp.exp2((t - mx) * c2)
        sm = jnp.sum(ps, axis=1, keepdims=True) + jnp.sum(pt, axis=1, keepdims=True)
        mix = jnp.dot(ps.astype(BF16), pv[:, cs], preferred_element_type=F32)
        mix = mix + jnp.dot(
            pt.astype(BF16), dv_pad[:, cs].astype(BF16), preferred_element_type=F32
        )
        priv_send[g, :, 0:HD] = mix
        priv_send[g, :, HD:] = jnp.where(lane == 0, mx, sm)

    def own_rows(b):
        return pl.ds(pl.multiple_of(b * lr, lr), lr)

    p_sends = []
    for off in range(1, n):
        to = lax.rem(me + off, n)
        p_sends.append(
            remote(
                priv_send.at[to // blocks, own_rows(to % blocks)], priv_buf.at[here],
                p_ssem.at[off], p_rsem.at[me], to,
            )
        )
        p_sends[-1].start()
    priv_buf[here] = priv_send[g_me, own_rows(b_me), :]

    for off in range(1, n):
        src = lax.rem(me + off, n)
        remote(qs.at[0], qbuf.at[pos(src)], q_ssem.at[off], q_rsem.at[src], src).wait_recv()
    loads[2].wait()
    loads[3].wait()
    rows = n * gr
    rb = 128
    ch = 4096
    reqs = rb // gr
    lane_b = lax.broadcasted_iota(jnp.int32, (rb, HD), 1)

    def merge_copies(p):
        ps = pl.ds(p * rp, rp)
        copies = []
        for off in range(1, blocks):
            b_to = lax.rem(b_me + off, blocks)
            copies.append(
                remote(
                    part.at[ps, own_rows(b_to)], merge_buf.at[b_me, ps],
                    m_ssem.at[p, off], m_rsem.at[p, b_me], g_me * blocks + b_to,
                )
            )
        return copies

    def merge_send(p):
        for copy in merge_copies(p):
            copy.start()

    core = me % 2
    chip = me // 2
    line = chip // 2
    side = chip % 2
    lines = n // 4

    def dev(line_at, side_at, core_at):
        return (line_at * 2 + side_at) * 2 + core_at

    across = dev(line, 1 - side, core)
    partner = dev(line, side, 1 - core)
    along = [lax.rem(line + off, lines) for off in range(1, lines)]
    mine_z = [dev(at, side, core) for at in along]
    mine_y = [dev(at, 1 - side, core) for at in [line] + along]
    other = [dev(at, sd, 1 - core) for sd in (side, 1 - side) for at in [line] + along]

    def gather_copies(p):
        pairs = [(me, across)] + [(me, to) for to in mine_z] + [(me, partner)]
        for src in mine_z:
            pairs += [(src, across), (src, partner)]
        pairs += [(src, partner) for src in mine_y]
        return [
            remote(gat.at[p, src], gat.at[p, src], g_ssem.at[p, i], g_rsem.at[p, src], to)
            for i, (src, to) in enumerate(pairs)
        ]

    def arrived(p, src):
        remote(
            gat.at[p, src], gat.at[p, src], g_ssem.at[p, 0], g_rsem.at[p, src], partner
        ).wait_recv()

    def finish(p):
        if p == 0:
            for off in range(1, n):
                src = lax.rem(me + off, n)
                remote(
                    priv_send.at[0, own_rows(0)], priv_buf.at[pos(src)],
                    p_ssem.at[off], p_rsem.at[src], src,
                ).wait_recv()
        ps = pl.ds(p * rp, rp)
        pieces = [priv_buf[ps], part[ps, own_rows(b_me), :]]
        for off in range(1, blocks):
            b_src = lax.rem(b_me + off, blocks)
            remote(
                part.at[ps, own_rows(0)], merge_buf.at[b_src, ps],
                m_ssem.at[p, off], m_rsem.at[p, b_src], g_me * blocks + b_src,
            ).wait_recv()
            pieces.append(merge_buf[b_src, ps])
        pieces = [x.reshape(rp * lr, 2 * HD) for x in pieces]
        peak = functools.reduce(jnp.maximum, [x[:, HD : HD + 1] for x in pieces])
        facs = [jnp.exp2((x[:, HD : HD + 1] - peak) * c2) for x in pieces]
        den = sum(f * x[:, HD + 1 : HD + 2] for f, x in zip(facs, pieces))
        num = sum(f * x[:, 0:HD] for f, x in zip(facs, pieces))
        fin[...] = (num / den).reshape(rp, lr, HD)
        for r in range(rp):
            for h in range(lh):
                att[r * draft : (r + 1) * draft, h * HD : (h + 1) * HD] = fin[
                    r, h * draft : (h + 1) * draft, :
                ]
        gat[p, me] = att[...].astype(BF16)
        for copy in gather_copies(p)[: lines + 1]:
            copy.start()

    def block(r, _):
        at = pl.ds(pl.multiple_of(r * reqs, reqs), reqs)
        qr = qbuf[at].reshape(rb, HD)
        peaks, mixes = [], []
        for c in range(k.shape[0] // ch):
            s = lax.dot_general(
                qr, k[c * ch : (c + 1) * ch, :], nt, preferred_element_type=F32
            )
            peaks.append(jnp.max(s, axis=1, keepdims=True))
            p = jnp.exp2((s - peaks[-1]) * c2).astype(BF16)
            mixes.append(jnp.dot(p, v[c * ch : (c + 1) * ch, :], preferred_element_type=F32))
        peak = functools.reduce(jnp.maximum, peaks)
        mix = sum(jnp.exp2((a - peak) * c2) * b for a, b in zip(peaks, mixes))
        part[at, :, 0:HD] = mix[:, 0:HD].reshape(reqs, gr, HD)
        part[at, :, HD:] = jnp.where(lane_b == 0, peak, mix[:, HD:]).reshape(reqs, gr, HD)

        @pl.when(r == half - 1)
        def _():
            merge_send(0)

        @pl.when(r == half)
        def _():
            finish(0)

        return 0

    half = rows // rb // PARTS
    lax.fori_loop(0, rows // rb, block, 0)

    def project(p, sources):
        total = None
        for src in sources:
            ws = pl.ds(pl.multiple_of(src * lc, lc), lc)
            one = jnp.dot(gat[p, src], w[ws, :], preferred_element_type=F32)
            total = one if total is None else total + one
        return total

    def forward_z(p):
        copies = gather_copies(p)[lines + 1 :]
        for i, src in enumerate(mine_z):
            arrived(p, src)
            copies[2 * i].start()
            copies[2 * i + 1].start()

    def forward_y(p):
        copies = gather_copies(p)[lines + 1 + 2 * len(mine_z) :]
        for i, src in enumerate(mine_y):
            arrived(p, src)
            copies[i].start()

    def out_copy(to, at):
        return remote(col.at[at], obuf.at[me], o_ssem.at[to], o_rsem.at[me], to)

    def out_send(p, total):
        for j in range(rp):
            q = p * rp + j
            for c in range(cols // HD):
                col_f[q, c * draft : (c + 1) * draft, :] = total[
                    j * draft : (j + 1) * draft, c * HD : (c + 1) * HD
                ]
            col[q] = col_f[q].astype(BF16)
        for j in range(rp):
            to = j * PARTS + p

            @pl.when(to != me)
            def _():
                out_copy(to, p * rp + j).start()

    merge_send(1)
    forward_z(0)
    finish(1)
    forward_y(0)
    loads[4].wait()
    total_0 = project(0, [me] + mine_z)
    forward_z(1)
    total_0 = total_0 + project(0, mine_y)
    for src in other:
        arrived(0, src)
    out_send(0, total_0 + project(0, other))
    total_1 = project(1, [me] + mine_z)
    forward_y(1)
    total_1 = total_1 + project(1, mine_y)
    for src in other:
        arrived(1, src)
    out_send(1, total_1 + project(1, other))
    obuf[me] = col[here]
    for off in range(1, n):
        src = lax.rem(me + off, n)
        remote(col.at[0], obuf.at[src], o_ssem.at[src], o_rsem.at[src], src).wait_recv()
    for src in range(n):
        got = obuf[src].astype(F32)
        for c in range(cols // HD):
            o_ref[:, src * cols + c * HD : src * cols + (c + 1) * HD] = got[
                c * draft : (c + 1) * draft, :
            ]
    for sends in (q_sends, p_sends):
        for send in sends:
            send.wait_send()
    for p in range(PARTS):
        for copy in merge_copies(p) + gather_copies(p):
            copy.wait_send()
    for off in range(1, n):
        out_copy(lax.rem(me + off, n), 0).wait_send()


def shards(
    n, queries, draft_keys, draft_values, parents, private_keys, private_values,
    priv_lengths, prefix_keys, prefix_values, out_weight,
):
    blocks = n // KVH
    lh = HEADS // n
    draft = queries.shape[0]
    gr = GH * draft
    lr = lh * draft
    slots = private_keys.shape[1]
    span = prefix_keys.shape[1]
    d, cols = out_weight.shape
    out_rows = max(16, draft * cols // HD)
    vm = pl.BlockSpec(memory_space=pltpu.VMEM)
    sm = pl.BlockSpec(memory_space=pltpu.SMEM)
    hb = pl.BlockSpec(memory_space=pl.ANY)
    dma = pltpu.SemaphoreType.DMA
    return pl.pallas_call(
        functools.partial(kernel, n),
        out_shape=jax.ShapeDtypeStruct((draft, n * cols), F32),
        in_specs=[vm, vm, vm, sm, sm, hb, hb, hb, hb, hb],
        out_specs=vm,
        scratch_shapes=[
            pltpu.VMEM((slots, KVH * HD), BF16),
            pltpu.VMEM((slots, KVH * HD), BF16),
            pltpu.VMEM((span, HD), BF16),
            pltpu.VMEM((span, 2 * HD), BF16),
            pltpu.VMEM((d, cols), BF16),
            pltpu.VMEM((KVH, gr, HD), F32),
            pltpu.VMEM((KVH, gr, HD), BF16),
            pltpu.VMEM((n, gr, HD), BF16),
            pltpu.VMEM((16, KVH * HD), F32),
            pltpu.VMEM((16, KVH * HD), F32),
            pltpu.VMEM((KVH, gr, 2 * HD), F32),
            pltpu.VMEM((n, lr, 2 * HD), F32),
            pltpu.VMEM((n, gr, 2 * HD), F32),
            pltpu.VMEM((blocks, n, lr, 2 * HD), F32),
            pltpu.VMEM((n // PARTS, lr, HD), F32),
            pltpu.VMEM((n // PARTS * draft, lh * HD), F32),
            pltpu.VMEM((PARTS, n, n // PARTS * draft, lh * HD), BF16),
            pltpu.VMEM((n, out_rows, HD), F32),
            pltpu.VMEM((n, out_rows, HD), BF16),
            pltpu.VMEM((n, out_rows, HD), BF16),
            dma((5,)),
            dma((n,)), dma((n,)), dma((n,)), dma((n,)),
            dma((PARTS, blocks)), dma((PARTS, blocks)),
            dma((PARTS, n)), dma((PARTS, n)), dma((n,)), dma((n,)),
        ],
        compiler_params=pltpu.CompilerParams(
            collective_id=0, has_side_effects=True, vmem_limit_bytes=58 << 20
        ),
        cost_estimate=pl.CostEstimate(
            flops=4 * n * gr * span * HD, bytes_accessed=24 << 20, transcendentals=n * gr * span
        ),
    )(
        queries, draft_keys, draft_values, parents, priv_lengths,
        private_keys, private_values, prefix_keys, prefix_values, out_weight,
    )


def solution(mesh):
    both = ("groups", "seq")
    in_specs = (
        P(both, None), P(both, None), P(both, None), P(both),
        P(both, None, None), P(both, None, None), P(both),
        P(both, None, None), P(both, None, None), P(None, "seq"),
    )
    return jax.shard_map(
        functools.partial(shards, mesh.shape["seq"]),
        mesh=mesh, in_specs=in_specs, out_specs=P(both, None), check_vma=False,
    )
```

time: 53.4 us -> 44.4 us (0.83)
  Pallas kernels: 50.7 us -> 42 us
    pallas_call x1, Pallas kernels: 50.7 us -> 42 us  [shards(): pl.pallas_call(functools.partial(kernel, n), out_shape=jax.ShapeDtypeStru...]
where the time goes in v2:
time: 44.4 us; the launch traced here: 44.2 us
  Pallas kernels  42 us (95%)
  local copies, waits for them, and re-layouts  1.57 us (4%)
  between operations  0.66 us (1%)
    pallas_call x1, Pallas kernels, shards(): pl.pallas_call(functools.partial(kernel, n), out_shape=jax.ShapeDtypeStru...  42 us
    unnamed x1, local copies, waits for them, and re-layouts  1.57 us

profile of v2, /device:TPU:1, one launch (start us, length us, event | category | flops | bytes accessed | tf_op | source)
XLA Modules:
  0.0 44.2 jit_solution(15764963377499720447)
XLA Ops:
  0.7 42.0 %shard_map.100 = f32[4,8192]{1,0:T(4,128)} custom-call(bf16[4,8192]{1,0:T(4,128)(2,1)} %q_ref.1, bf16[4,1024]{1,0:T(4,128)(2,1)} %dk_ref.1, bf16[4,1024]{1,0:T(4,128)(2,1)} %dv_ref.1, s32[4]{0:T(128)} %par_ref.1, s32[1]{0:T(128)S(6)} %copy.12.len_ref, bf16[1,1024,1024]{2,1,0:T(8,128)(2,1)} %pk_hbm.1, bf16[1,1024,1024]{2,1,0:T(8,128)(2,1)} %pv_hbm.1, ...), custom_call_target="tpu_custom_call" | custom-call | flops 4294967296 | bytes 25165824 | tf_op jit(solution)/shard_map/pallas_call | solution.py:394
  42.6 1.6 %copy.13 = f32[4,8192]{1,0:T(4,128)} copy(f32[4,8192]{1,0:T(4,128)} %shard_map.100) | data formatting | bytes 262144

commit v3 on v2

--- a/solution.py
+++ b/solution.py
@@ -185,7 +185,7 @@
     loads[3].wait()
     rows = n * gr
     rb = 128
-    ch = 4096
+    ch = 2048
     reqs = rb // gr
     lane_b = lax.broadcasted_iota(jnp.int32, (rb, HD), 1)
 

time: 44.4 us -> 43.6 us (0.982)
  Pallas kernels: 42 us -> 41.2 us
    pallas_call x1, Pallas kernels: 42 us -> 41.2 us  [shards(): pl.pallas_call(functools.partial(kernel, n), out_shape=jax.ShapeDtypeStru...]
where the time goes in v3:
time: 43.6 us; the launch traced here: 43.4 us
  Pallas kernels  41.2 us (94%)
  local copies, waits for them, and re-layouts  1.57 us (4%)
  between operations  0.66 us (2%)
    pallas_call x1, Pallas kernels, shards(): pl.pallas_call(functools.partial(kernel, n), out_shape=jax.ShapeDtypeStru...  41.2 us
    unnamed x1, local copies, waits for them, and re-layouts  1.57 us

profile of v3, /device:TPU:1, one launch (start us, length us, event | category | flops | bytes accessed | tf_op | source)
XLA Modules:
  0.0 43.4 jit_solution(1693916155627720878)
XLA Ops:
  0.7 41.2 %shard_map.100 = f32[4,8192]{1,0:T(4,128)} custom-call(bf16[4,8192]{1,0:T(4,128)(2,1)} %q_ref.1, bf16[4,1024]{1,0:T(4,128)(2,1)} %dk_ref.1, bf16[4,1024]{1,0:T(4,128)(2,1)} %dv_ref.1, s32[4]{0:T(128)} %par_ref.1, s32[1]{0:T(128)S(6)} %copy.12.len_ref, bf16[1,1024,1024]{2,1,0:T(8,128)(2,1)} %pk_hbm.1, bf16[1,1024,1024]{2,1,0:T(8,128)(2,1)} %pv_hbm.1, ...), custom_call_target="tpu_custom_call" | custom-call | flops 4294967296 | bytes 25165824 | tf_op jit(solution)/shard_map/pallas_call | solution.py:394
  41.9 1.6 %copy.13 = f32[4,8192]{1,0:T(4,128)} copy(f32[4,8192]{1,0:T(4,128)} %shard_map.100) | data formatting | bytes 262144
